TPU v7x, 256 devices: a whole 4x4x8 slice. The times are simulated.
256 devices in a mesh: dp: 32 (over x, z_hi, core), layer: 8 (over y, z_lo).
Axes of the slice: x: 4, y: 4, z: 8 (z_hi: 4, z_lo: 2; z = z_hi * 2 + z_lo), core: 2. Of those that a mesh axis runs over, the one named last changes fastest.
Arguments:
- grads: bfloat16 [8, 16384, 1024], P('layer', 'dp'), as said below
- damping_level: int32 [8], P('layer'), may hold values from 0 to 4, as said below
- pair_blocks: int32 [2048, 2], P('dp'), may hold values from -1 to 127, as said below
Outputs:
- tiles: float32 [2048, 128, 128], P(('dp', 'layer'))
Inputs may be any that keep to these rules, and one draw needn't show every extreme that they name: `grads`: gradients of order one, finite. `damping_level`: consecutive layers have different levels. `pair_blocks`: row r is owned by shard r // 64, which holds blocks of that shard index times 4 onward; the first entry is one of the owner's blocks. The second is -1 for an empty slot, else a block of shard (owner + s) mod the number of dp shards with 1 <= s <= 4. The first slot of every owner is live with s = 4; the live slots of an owner come first, and some owner has no empty slot.
All inputs are finite; a program needn't handle non-finite values.
Results may differ from a plain program's by a relative error of at most 0.0042.
Values may be sent and summed in bfloat16 or wider, within the bound.
No kernel may reach another device: no remote copies, remote signals or barrier semaphores. Data moves between devices by JAX's collectives and lax.ppermute only.
A program may use at most 128 MiB of HBM per device.

v0:
```python
import math

import jax
import jax.numpy as jnp
from jax import lax
from jax.sharding import PartitionSpec as P

BLOCK = 128
REACH = 4


def passed_along(value, axis, steps):
    count = lax.axis_size(axis)
    pairs = [(source, (source + steps) % count) for source in range(count)]
    return lax.ppermute(value, axis, pairs)


def shards(grads, damping_level, pair_blocks):
    layer_dev, doc_dev, width = grads.shape
    blocks_dev = doc_dev // BLOCK
    dp_count = lax.axis_size("dp")
    total_docs = doc_dev * dp_count
    total_layers = layer_dev * lax.axis_size("layer")
    local_cov = jnp.einsum("ldp,ldq->lpq", grads, grads, preferred_element_type=jnp.float32)
    summed = lax.psum(local_cov, "dp")
    damping = 0.05 * jnp.exp2(damping_level.astype(jnp.float32))
    covariance = summed / total_docs + damping[:, None, None] * jnp.eye(width, dtype=jnp.float32)
    factor = jnp.linalg.cholesky(covariance)
    solved = lax.linalg.triangular_solve(
        factor, jnp.swapaxes(grads.astype(jnp.float32), 1, 2), left_side=True, lower=True
    )
    whitened = jnp.swapaxes(solved, 1, 2).astype(jnp.bfloat16)
    shard_index = lax.axis_index("dp")
    first_block = pair_blocks[:, 0]
    second_raw = pair_blocks[:, 1]
    live_slot = second_raw >= 0
    second_block = jnp.maximum(second_raw, 0)
    local_first = first_block - shard_index * blocks_dev
    distance = (second_block // blocks_dev - shard_index) % dp_count
    column = second_block % blocks_dev
    own_blocks = whitened.reshape(layer_dev, blocks_dev, BLOCK, width)
    first_rows = jnp.take(own_blocks, local_first, axis=1)
    arrivals = []
    for offset in range(1, REACH + 1):
        arrivals.append(passed_along(whitened, "dp", -offset))
    neighbours = jnp.concatenate(arrivals, 1).reshape(layer_dev, REACH * blocks_dev, BLOCK, width)
    pick_index = jnp.clip((distance - 1) * blocks_dev + column, 0, REACH * blocks_dev - 1)
    partner = jnp.take(neighbours, pick_index, axis=1)
    scale = 1.0 / math.sqrt(width * total_layers)
    products = (
        jnp.einsum("lkip,lkjp->kij", first_rows, partner, preferred_element_type=jnp.float32)
        * scale
    )
    products = jnp.where(live_slot[:, None, None], products, 0.0)
    return lax.psum_scatter(products, "layer", scatter_dimension=0, tiled=True)


def solution(mesh):
    return jax.shard_map(
        shards,
        mesh=mesh,
        in_specs=(P("layer", "dp", None), P("layer"), P("dp", None)),
        out_specs=P(("dp", "layer"), None, None),
        check_vma=False,
    )
```

profile of v0, /device:TPU:1, one launch (start us, length us, event | category | flops | bytes accessed | tf_op | source)
XLA Modules:
  0.0 979.2 jit_solution(6103406875681619458)
XLA Ops:
  13.6 299.7 %all-reduce.3.cloned.1.call-done = f32[1,1024,1024]{1,2,0:T(8,128)} async-done(((f32[1,1024,1024]{1,2,0:T(8,128)}), f32[1,1024,1024]{1,2,0:T(8,128)}) %all-reduce.3.cloned.1.call-update) | async-done | bytes 4194320 | tf_op jit(solution)/shard_map/psum | solution.py:25
  330.6 11.7 %custom-call.70 = f32[1,128,128]{2,1,0:T(8,128)S(1)} custom-call(f32[1,128,128]{2,1,0:T(8,128)S(1)} %cholesky.582), custom_call_target="Cholesky" | custom-call | tf_op jit(solution)/shard_map/jit(cholesky)/cholesky | solution.py:28
  342.5 9.8 %custom-call.71 = f32[1,1,128,128]{2,3,1,0:T(8,128)S(1)} custom-call(f32[1,1,128,128]{3,2,1,0:T(8,128)S(1)} %get-tuple-element.65), custom_call_target="InvertDiagBlocksLowerTriangular" | custom-call | tf_op jit(solution)/shard_map/jit(cholesky)/cholesky | solution.py:28
  359.1 11.7 %custom-call.72 = f32[1,128,128]{2,1,0:T(8,128)S(1)} custom-call(f32[1,128,128]{2,1,0:T(8,128)S(1)} %cholesky.586), custom_call_target="Cholesky" | custom-call | tf_op jit(solution)/shard_map/jit(cholesky)/cholesky | solution.py:28
  371.1 9.8 %custom-call.73 = f32[1,1,128,128]{2,3,1,0:T(8,128)S(1)} custom-call(f32[1,1,128,128]{3,2,1,0:T(8,128)S(1)} %get-tuple-element.63), custom_call_target="InvertDiagBlocksLowerTriangular" | custom-call | tf_op jit(solution)/shard_map/jit(cholesky)/cholesky | solution.py:28
  387.8 11.7 %custom-call.74 = f32[1,128,128]{2,1,0:T(8,128)S(1)} custom-call(f32[1,128,128]{2,1,0:T(8,128)S(1)} %cholesky.591), custom_call_target="Cholesky" | custom-call | tf_op jit(solution)/shard_map/jit(cholesky)/cholesky | solution.py:28
  400.3 9.8 %custom-call.75 = f32[1,1,128,128]{2,3,1,0:T(8,128)S(1)} custom-call(f32[1,1,128,128]{3,2,1,0:T(8,128)S(1)} %get-tuple-element.61), custom_call_target="InvertDiagBlocksLowerTriangular" | custom-call | tf_op jit(solution)/shard_map/jit(cholesky)/cholesky | solution.py:28
  416.5 11.7 %custom-call.76 = f32[1,128,128]{2,1,0:T(8,128)S(1)} custom-call(f32[1,128,128]{2,1,0:T(8,128)S(1)} %cholesky.596), custom_call_target="Cholesky" | custom-call | tf_op jit(solution)/shard_map/jit(cholesky)/cholesky | solution.py:28
  429.0 9.8 %custom-call.77 = f32[1,1,128,128]{2,3,1,0:T(8,128)S(1)} custom-call(f32[1,1,128,128]{3,2,1,0:T(8,128)S(1)} %get-tuple-element.59), custom_call_target="InvertDiagBlocksLowerTriangular" | custom-call | tf_op jit(solution)/shard_map/jit(cholesky)/cholesky | solution.py:28
  444.0 12.1 %custom-call.78 = f32[1,128,128]{2,1,0:T(8,128)S(1)} custom-call(f32[1,128,128]{2,1,0:T(8,128)S(1)} %cholesky.601), custom_call_target="Cholesky" | custom-call | tf_op jit(solution)/shard_map/jit(cholesky)/cholesky | solution.py:28
  458.0 10.6 %custom-call.79 = f32[1,1,128,128]{2,3,1,0:T(8,128)S(1)} custom-call(f32[1,1,128,128]{3,2,1,0:T(8,128)} %get-tuple-element.57), custom_call_target="InvertDiagBlocksLowerTriangular" | custom-call | tf_op jit(solution)/shard_map/jit(cholesky)/cholesky | solution.py:28
  472.8 11.7 %custom-call.80 = f32[1,128,128]{2,1,0:T(8,128)S(1)} custom-call(f32[1,128,128]{2,1,0:T(8,128)S(1)} %cholesky.606), custom_call_target="Cholesky" | custom-call | tf_op jit(solution)/shard_map/jit(cholesky)/cholesky | solution.py:28
  485.8 9.8 %custom-call.81 = f32[1,1,128,128]{2,3,1,0:T(8,128)S(1)} custom-call(f32[1,1,128,128]{3,2,1,0:T(8,128)S(1)} %get-tuple-element.55), custom_call_target="InvertDiagBlocksLowerTriangular" | custom-call | tf_op jit(solution)/shard_map/jit(cholesky)/cholesky | solution.py:28
  499.5 11.7 %custom-call.82 = f32[1,128,128]{2,1,0:T(8,128)S(1)} custom-call(f32[1,128,128]{2,1,0:T(8,128)S(1)} %cholesky.611), custom_call_target="Cholesky" | custom-call | tf_op jit(solution)/shard_map/jit(cholesky)/cholesky | solution.py:28
  512.0 9.8 %custom-call.83 = f32[1,1,128,128]{2,3,1,0:T(8,128)S(1)} custom-call(f32[1,1,128,128]{3,2,1,0:T(8,128)S(1)} %get-tuple-element.53), custom_call_target="InvertDiagBlocksLowerTriangular" | custom-call | tf_op jit(solution)/shard_map/jit(cholesky)/cholesky | solution.py:28
  524.8 11.7 %custom-call.84 = f32[1,128,128]{2,1,0:T(8,128)S(1)} custom-call(f32[1,128,128]{2,1,0:T(8,128)S(1)} %fusion.66), custom_call_target="Cholesky" | custom-call | tf_op jit(solution)/shard_map/jit(cholesky)/cholesky | solution.py:28
  552.7 28.8 %while.1 = (s32[]{:T(128)}, f32[1,1024,1024]{1,2,0:T(8,128)}, s32[8,2]{0,1:T(2,128)S(1)}, f32[8,1,128,128]{3,2,1,0:T(8,128)}, s32[]{:T(128)}) while((s32[]{:T(128)}, f32[1,1024,1024]{1,2,0:T(8,128)}, s32[8,2]{0,1:T(2,128)S(1)}, f32[8,1,128,128]{3,2,1,0:T(8,128)}, s32[]{:T(128)}) %tuple.54), condition=%wide.while_cond, body=%wide.while_body.sunk | while | flops 2 | bytes 393333 | solution.py:29
  581.5 80.0 %custom-call.85 = f32[1,8,128,128]{2,3,1,0:T(8,128)} custom-call(f32[1,8,128,128]{3,2,1,0:T(8,128)} %bitcast.375), custom_call_target="InvertDiagBlocksLowerTriangular" | custom-call | tf_op jit(solution)/shard_map/triangular_solve | solution.py:29
  700.1 45.1 %collective-permute-done.3 = bf16[1,512,1024]{1,2,0:T(8,128)(2,1)S(1)} collective-permute-done((bf16[1,512,1024]{1,2,0:T(8,128)(2,1)}, bf16[1,512,1024]{1,2,0:T(8,128)(2,1)S(1)}, u32[]{:S(2)}, u32[]{:S(2)}) %collective-permute-start.3) | collective-permute-done | bytes 1048608 | tf_op jit(solution)/shard_map/ppermute | solution.py:15
  745.2 77.1 %collective-permute-done.2 = bf16[1,512,1024]{1,2,0:T(8,128)(2,1)S(1)} collective-permute-done((bf16[1,512,1024]{1,2,0:T(8,128)(2,1)}, bf16[1,512,1024]{1,2,0:T(8,128)(2,1)S(1)}, u32[]{:S(2)}, u32[]{:S(2)}) %collective-permute-start.2) | collective-permute-done | bytes 1048608 | tf_op jit(solution)/shard_map/ppermute | solution.py:15
  822.3 23.2 %collective-permute-done.1 = bf16[1,512,1024]{1,2,0:T(8,128)(2,1)} collective-permute-done((bf16[1,512,1024]{1,2,0:T(8,128)(2,1)}, bf16[1,512,1024]{1,2,0:T(8,128)(2,1)}, u32[]{:S(2)}, u32[]{:S(2)}) %collective-permute-start.1) | collective-permute-done | bytes 1048608 | tf_op jit(solution)/shard_map/ppermute | solution.py:15
  857.9 9.7 gather_fusion.1
  867.6 14.5 %multiply_select_fusion = f32[64,128,128]{2,1,0:T(8,128)} fusion(bf16[64,128,1024]{2,1,0:T(8,128)(2,1)} %gather_fusion.1, pred[64]{0:T(512)(128)(4,1)S(1)} %get-tuple-element.68, bf16[64,128,1024]{2,1,0:T(8,128)(2,1)} %gather_fusion, pred[64]{0:T(512)(128)(4,1)S(1)} %get-tuple-element.29, pred[64]{0:T(512)(128)(4,1)S(1)} %get-tuple-element.67), kind=kOutput, calls=%fused_computation.15 | convolution fusion | flops 2166358016 | bytes 37748928 | tf_op jit(solution)/shard_map/lkip,lkjp->kij/dot_general | solution.py:51
  882.1 90.0 %reduce-scatter.2.cloned.1.call-done = f32[8,128,128]{2,1,0:T(8,128)} async-done(((f32[64,128,128]{2,1,0:T(8,128)}), f32[8,128,128]{2,1,0:T(8,128)}) %reduce-scatter.2.cloned.1.call-update) | async-done | bytes 524304 | tf_op jit(solution)/shard_map/reduce_scatter | solution.py:55
  (163 shorter events, 156.3 us)
Async XLA Ops:
  6.5 5.0 copy-start.7
  6.5 306.8 %all-reduce.3.cloned.1.call-start = ((), (), s32[]{:S(2)}) async-start(), calls=%async_computation.1 | async-start | bytes 8388608 | tf_op jit(solution)/shard_map/psum | solution.py:25
  11.5 960.7 %reduce-scatter.2.cloned.1.call-start = ((), (), s32[]{:S(2)}) async-start(), calls=%async_computation.2 | async-start | bytes 4718592 | tf_op jit(solution)/shard_map/reduce_scatter | solution.py:55
  328.7 1.9 copy-start.1
  358.3 0.8 copy-start.3
  380.9 1.0 copy-start.2
  381.0 1.2 copy-start.4
  382.6 2.0 copy-start
  387.0 0.8 copy-start.5
  415.7 0.8 copy-start.6
  547.8 4.8 copy-start.10
  661.5 6.5 copy-start.8
  676.9 14.2 %copy-start.9 = (s32[64,2]{0,1:T(2,128)S(1)}, s32[64,2]{0,1:T(2,128)}, u32[]{:S(2)}) copy-start(s32[64,2]{0,1:T(2,128)} %param.5) | copy-start | bytes 1540
  684.6 60.6 %collective-permute-start.3 = (bf16[1,512,1024]{1,2,0:T(8,128)(2,1)}, bf16[1,512,1024]{1,2,0:T(8,128)(2,1)S(1)}, u32[]{:S(2)}, u32[]{:S(2)}) collective-permute-start(bf16[1,512,1024]{1,2,0:T(8,128)(2,1)} %bitcast.99), channel_id=1, source_target_pairs={{0,224},{8,232},{16,240},{24,248},{32,0},{40,8},{48,16},{56,24},{6... | collective-permute-start | bytes 3145736 | tf_op jit(solution)/shard_map/ppermute | solution.py:15
  687.4 134.8 %collective-permute-start.2 = (bf16[1,512,1024]{1,2,0:T(8,128)(2,1)}, bf16[1,512,1024]{1,2,0:T(8,128)(2,1)S(1)}, u32[]{:S(2)}, u32[]{:S(2)}) collective-permute-start(bf16[1,512,1024]{1,2,0:T(8,128)(2,1)} %bitcast.99), channel_id=1, source_target_pairs={{0,232},{8,240},{16,248},{24,0},{32,8},{40,16},{48,24},{56,32},{64... | collective-permute-start | bytes 3145736 | tf_op jit(solution)/shard_map/ppermute | solution.py:15
  687.4 158.1 %collective-permute-start.1 = (bf16[1,512,1024]{1,2,0:T(8,128)(2,1)}, bf16[1,512,1024]{1,2,0:T(8,128)(2,1)}, u32[]{:S(2)}, u32[]{:S(2)}) collective-permute-start(bf16[1,512,1024]{1,2,0:T(8,128)(2,1)} %bitcast.99), channel_id=1, source_target_pairs={{0,240},{8,248},{16,0},{24,8},{32,16},{40,24},{48,32},{56,40},{64,... | collective-permute-start | bytes 3145736 | tf_op jit(solution)/shard_map/ppermute | solution.py:15
  691.1 157.0 %collective-permute-start = (bf16[1,512,1024]{1,2,0:T(8,128)(2,1)}, bf16[1,512,1024]{1,2,0:T(8,128)(2,1)}, u32[]{:S(2)}, u32[]{:S(2)}) collective-permute-start(bf16[1,512,1024]{1,2,0:T(8,128)(2,1)} %bitcast.99), channel_id=1, source_target_pairs={{0,248},{8,0},{16,8},{24,16},{32,24},{40,32},{48,40},{56,48},{64,5... | collective-permute-start | bytes 3145736 | tf_op jit(solution)/shard_map/ppermute | solution.py:15
Sparse Core Ops, SparseCore 0:
  11.6 301.7 all-reduce.2
  882.3 89.8 reduce-scatter.1
where the time goes:
time: 983 us; the launch traced here: 979 us
  waiting for transfers between devices  538 us (55%)
  other arithmetic  270 us (27%)
  local copies, waits for them, and re-layouts  74.6 us (8%)
  matrix products  70.6 us (7%)
  between operations  19.7 us (2%)
    psum x1, waiting for transfers between devices, shards(): summed = lax.psum(local_cov, 'dp')  300 us
    another operation x30, other arithmetic, shards(): factor = jnp.linalg.cholesky(covariance)  171 us
    ppermute x4, waiting for transfers between devices, passed_along(): return lax.ppermute(value, axis, pairs)  148 us
    reduce_scatter x1, waiting for transfers between devices, shards(): return lax.psum_scatter(products, 'layer', scatter_dimension=0, tiled=True)  90 us
    another operation x3, other arithmetic, shards(): lax.linalg.triangular_solve(factor, jnp.swapaxes(grads.astype(jnp.float32...  85.4 us
    another operation x14, matrix products, shards(): factor = jnp.linalg.cholesky(covariance)  28.8 us
    another operation x40, local copies, waits for them, and re-layouts  28.5 us
    another operation x15, matrix products, shards(): lax.linalg.triangular_solve(factor, jnp.swapaxes(grads.astype(jnp.float32...  22.4 us
  transfers between devices with their start and end apart: 6, of which 6 were waited for; matrix products, arithmetic and copies ran while one was open for 1% of the time, Pallas kernels for 0%

commit v1 on v0

v1 whole, which is shorter than its diff:
```python
import math

import jax
import jax.numpy as jnp
from jax import lax
from jax.experimental import pallas as pl
from jax.experimental.pallas import tpu as pltpu
from jax.sharding import PartitionSpec as P

BLOCK = 128
PIVOT = 256
PIVOTS = 4
WIDTH = PIVOT * PIVOTS
DOC_DEV = 512
DOCS = 16384
REACH = 4
HALF_ROWS = 18 * BLOCK
X_ROWS = HALF_ROWS // 4
Z_ROWS = X_ROWS // 4
SOURCES = 5
TOLERANCE = 3e-3
MAX_STEPS = 60
OFF_PLACE = {(1, 0): (0, 0), (2, 0): (0, 1), (3, 0): (0, 2), (2, 1): (1, 0), (3, 1): (1, 1), (3, 2): (1, 2)}

f32 = jnp.float32
bf16 = jnp.bfloat16


def dot(a, b, contract=((1,), (0,))):
    return lax.dot_general(
        a, b, (contract, ((), ())), precision=lax.Precision.HIGHEST, preferred_element_type=f32
    )


def dot16(a, b, contract=((1,), (0,))):
    return lax.dot_general(a, b, (contract, ((), ())), preferred_element_type=f32)


def move(value, dx=0, dz=0, dcore=0, chips=0):
    pairs = []
    for i in range(32):
        x, z, core = i // 8, (i // 2) % 4, i % 2
        chip = ((x + dx) % 4) * 4 + (z + dz) % 4
        pairs.append((i, ((chip + chips) % 16) * 2 + (core + dcore) % 2))
    return lax.ppermute(value, "dp", pairs)


def covariance_kernel(index_ref, g_ref, s_ref, out_ref):
    def product(place):
        i = pl.multiple_of(index_ref[2 * place] * PIVOT, PIVOT)
        j = pl.multiple_of(index_ref[2 * place + 1] * PIVOT, PIVOT)
        return dot16(g_ref[:, pl.ds(i, PIVOT)], g_ref[:, pl.ds(j, PIVOT)], ((0,), (0,))) + dot16(
            s_ref[:, pl.ds(i, PIVOT)], s_ref[:, pl.ds(j, PIVOT)], ((0,), (0,))
        )

    row = 0
    for place in range(5):
        block = product(place)
        for r, c in ((0, 0), (0, 1), (1, 0), (1, 1)):
            if place >= 3 and (r, c) == (0, 1):
                continue
            out_ref[row : row + BLOCK, :] = block[r * BLOCK : (r + 1) * BLOCK, c * BLOCK : (c + 1) * BLOCK]
            row += BLOCK


def covariance_half(g, sibling, core):
    first = jnp.array([1, 0, 2, 0, 3, 0, 0, 0, 1, 1], jnp.int32)
    second = jnp.array([2, 1, 3, 1, 3, 2, 2, 2, 3, 3], jnp.int32)
    index = jnp.where(core == 0, first, second)
    return pl.pallas_call(
        covariance_kernel,
        out_shape=jax.ShapeDtypeStruct((HALF_ROWS, BLOCK), f32),
        in_specs=[
            pl.BlockSpec(memory_space=pltpu.SMEM),
            pl.BlockSpec(memory_space=pltpu.VMEM),
            pl.BlockSpec(memory_space=pltpu.VMEM),
        ],
        out_specs=pl.BlockSpec(memory_space=pltpu.VMEM),
        compiler_params=pltpu.CompilerParams(vmem_limit_bytes=32 * 2**20),
        cost_estimate=pl.CostEstimate(flops=2 * 5 * PIVOT * PIVOT * 1024, bytes_accessed=4 * 2**20, transcendentals=0),
    )(index, g, sibling)


def norm(r):
    return jnp.max(jnp.sum(jnp.abs(r), axis=1, keepdims=True))


def invert(a, p_ref, m_ref, x_ref, r_ref):
    rows = lax.broadcasted_iota(jnp.int32, (PIVOT, PIVOT), 0)
    cols = lax.broadcasted_iota(jnp.int32, (PIVOT, PIVOT), 1)
    eye = jnp.where(rows == cols, 1.0, 0.0).astype(f32)
    diagonal = a * eye
    scale_row = lax.rsqrt(jnp.sum(diagonal, axis=0, keepdims=True))
    scale_col = lax.rsqrt(jnp.sum(diagonal, axis=1, keepdims=True))
    m = a * scale_row * scale_col
    m_ref[...] = m
    off = eye - m
    squared = dot(off, off)
    r_ref[...] = squared
    x_ref[...] = eye + off
    size = norm(squared)

    @pl.when(jnp.logical_not(size < 0.95))
    def _():
        step = 1.9 / norm(m)
        x = step * (2.0 * eye - step * m)
        x_ref[...] = x
        r_ref[...] = eye - dot(m, x)

    def unfinished(carry):
        size, count = carry
        return jnp.logical_and(size > TOLERANCE, count < MAX_STEPS)

    def improve(carry):
        _, count = carry
        x = x_ref[...] + dot(x_ref[...], r_ref[...])
        x_ref[...] = x
        r = eye - dot(m_ref[...], x)
        r_ref[...] = r
        return norm(r), count + 1

    lax.while_loop(unfinished, improve, (norm(r_ref[...]), jnp.int32(0)))
    x = x_ref[...] + dot(x_ref[...], r_ref[...])
    p_ref[...] = x * scale_row * scale_col


def solve_kernel(place_ref, level_ref, w_ref, s_ref, g_ref, out_ref, packed, c, low, p, y, m, x, r):
    mine_x, mine_z, core = place_ref[0], place_ref[1], place_ref[2]
    for half, ref in ((core, w_ref), (1 - core, s_ref)):
        for i in range(4):
            for j in range(4):
                row = half * HALF_ROWS + ((mine_x + i) % 4) * X_ROWS + ((mine_z + j) % 4) * Z_ROWS
                row = pl.multiple_of(row, 16)
                start = i * X_ROWS + j * Z_ROWS
                packed[pl.ds(row, Z_ROWS), :] = ref[start : start + Z_ROWS, :]

    rows = lax.broadcasted_iota(jnp.int32, (PIVOT, PIVOT), 0)
    cols = lax.broadcasted_iota(jnp.int32, (PIVOT, PIVOT), 1)
    level = jnp.full((PIVOT, PIVOT), level_ref[0], jnp.int32).astype(f32)
    damped = jnp.where(rows == cols, 0.05 * jnp.exp2(level), 0.0)

    def piece(half, place):
        start = half * HALF_ROWS + place * BLOCK
        return packed[start : start + BLOCK, :] * (1.0 / DOCS)

    for (i, j), (half, place) in OFF_PLACE.items():
        for t in range(4):
            c[i, j, (t // 2) * BLOCK : (t // 2 + 1) * BLOCK, (t % 2) * BLOCK : (t % 2 + 1) * BLOCK] = piece(
                half, 4 * place + t
            )
    for i in range(PIVOTS):
        half, place = i // 2, 12 + 3 * (i % 2)
        a, b, d = piece(half, place), piece(half, place + 1), piece(half, place + 2)
        top = jnp.concatenate([a, b.T], axis=1)
        bottom = jnp.concatenate([b, d], axis=1)
        c[i, i] = jnp.concatenate([top, bottom], axis=0) + damped
    for i in range(PIVOTS):
        y[i] = g_ref[:, i * PIVOT : (i + 1) * PIVOT].astype(f32)

    for k in range(PIVOTS):
        invert(c[k, k], p.at[k], m, x, r)
        for i in range(k + 1, PIVOTS):
            low[i, k] = dot(c[i, k], p[k])
        for i in range(k + 1, PIVOTS):
            for j in range(k + 1, i + 1):
                c[i, j] = c[i, j] - dot(low[i, k], c[j, k], ((1,), (1,)))
        for i in range(k + 1, PIVOTS):
            y[i] = y[i] - dot(y[k], low[i, k], ((1,), (1,)))
    scale = 1.0 / math.sqrt(WIDTH * 8)
    for k in range(PIVOTS - 1, -1, -1):
        h = dot(y[k], p[k])
        for i in range(k + 1, PIVOTS):
            h = h - dot(y[i], low[i, k])
        y[k] = h
        h = h * scale
        high = h.astype(bf16)
        rest = (h - high.astype(f32)).astype(bf16)
        for block in range(DOC_DEV // BLOCK):
            out_ref[block, :BLOCK, k * PIVOT : (k + 1) * PIVOT] = high[block * BLOCK : (block + 1) * BLOCK]
            out_ref[block, BLOCK:, k * PIVOT : (k + 1) * PIVOT] = rest[block * BLOCK : (block + 1) * BLOCK]


def solve(place, level, mine, other, g):
    smem, vmem = pl.BlockSpec(memory_space=pltpu.SMEM), pl.BlockSpec(memory_space=pltpu.VMEM)
    return pl.pallas_call(
        solve_kernel,
        out_shape=jax.ShapeDtypeStruct((DOC_DEV // BLOCK, 2 * BLOCK, WIDTH), bf16),
        in_specs=[smem, smem, vmem, vmem, vmem],
        out_specs=vmem,
        scratch_shapes=[
            pltpu.VMEM((2 * HALF_ROWS, BLOCK), f32),
            pltpu.VMEM((PIVOTS, PIVOTS, PIVOT, PIVOT), f32),
            pltpu.VMEM((PIVOTS, PIVOTS, PIVOT, PIVOT), f32),
            pltpu.VMEM((PIVOTS, PIVOT, PIVOT), f32),
            pltpu.VMEM((PIVOTS, DOC_DEV, PIVOT), f32),
            pltpu.VMEM((PIVOT, PIVOT), f32),
            pltpu.VMEM((PIVOT, PIVOT), f32),
            pltpu.VMEM((PIVOT, PIVOT), f32),
        ],
        compiler_params=pltpu.CompilerParams(vmem_limit_bytes=48 * 2**20),
        cost_estimate=pl.CostEstimate(flops=40 * 10**9, bytes_accessed=8 * 2**20, transcendentals=0),
    )(place, level, mine, other, g)


def tiles_kernel(pairs_ref, h_ref, *refs):
    sources, (out_ref, held, sems) = refs[:SOURCES], refs[SOURCES:]
    copies = [
        pltpu.make_async_copy(source, held.at[pl.ds(n * DOC_DEV, DOC_DEV)], sems.at[n])
        for n, source in enumerate(sources)
    ]
    for copy in copies:
        copy.start()
    for copy in copies:
        copy.wait()

    def one(n, carry):
        first, second, live = pairs_ref[0, n], pairs_ref[1, n], pairs_ref[2, n]
        partner = held[pl.ds(pl.multiple_of(second * BLOCK, BLOCK), BLOCK), :]
        both = dot16(h_ref[first], partner, ((1,), (1,)))
        tile = both[:BLOCK] + both[BLOCK:]
        out_ref[n] = jnp.where(live > 0, tile, 0.0).astype(bf16)
        return carry

    lax.fori_loop(0, out_ref.shape[0], one, 0, unroll=4)


def layer_tiles(pairs, h, sources):
    count = pairs.shape[1]
    return pl.pallas_call(
        tiles_kernel,
        out_shape=jax.ShapeDtypeStruct((count, BLOCK, BLOCK), bf16),
        in_specs=[pl.BlockSpec(memory_space=pltpu.SMEM), pl.BlockSpec(memory_space=pltpu.VMEM)]
        + [pl.BlockSpec(memory_space=pl.ANY)] * SOURCES,
        out_specs=pl.BlockSpec(memory_space=pltpu.VMEM),
        scratch_shapes=[pltpu.VMEM((SOURCES * DOC_DEV, WIDTH), bf16), pltpu.SemaphoreType.DMA((SOURCES,))],
        compiler_params=pltpu.CompilerParams(vmem_limit_bytes=32 * 2**20),
        cost_estimate=pl.CostEstimate(
            flops=4 * count * BLOCK * BLOCK * WIDTH, bytes_accessed=9 * 2**20, transcendentals=0
        ),
    )(pairs, h, *sources)


def shards(grads, damping_level, pair_blocks):
    g = grads[0]
    me = lax.axis_index("dp")
    mine_x, mine_z, core = me // 8, (me // 2) % 4, me % 2
    sibling = move(g, dcore=1)
    near = move(g, chips=-1)
    far = move(near, chips=-1)
    near_other = move(near, dcore=1)
    far_other = move(far, dcore=1)

    part = covariance_half(g, sibling, core)
    for position, rows, axis in ((mine_x, X_ROWS, "dx"), (mine_z, Z_ROWS, "dz")):
        cut = [lax.dynamic_slice_in_dim(part, ((position + s) % 4) * rows, rows) for s in range(4)]
        part = cut[0] + move(cut[1], **{axis: 1}) + move(cut[2], **{axis: 2}) + move(cut[3], **{axis: 3})
    for axis in ("dz", "dx"):
        part = jnp.concatenate([part] + [move(part, **{axis: -s}) for s in (1, 2, 3)])
    other = move(part, dcore=1)
    place = jnp.stack([mine_x, mine_z, core]).astype(jnp.int32)
    h = solve(place, damping_level, part, other, g)

    blocks_dev = DOC_DEV // BLOCK
    first, second = pair_blocks[:, 0], pair_blocks[:, 1]
    live = second >= 0
    second = jnp.maximum(second, 0)
    distance = jnp.clip((second // blocks_dev - me) % 32, 1, REACH) - 1
    source = jnp.where(core == 0, jnp.array([0, 1, 2, 3]), jnp.array([2, 1, 4, 3]))
    held_block = source[distance] * blocks_dev + second % blocks_dev
    pairs = jnp.stack([first - me * blocks_dev, held_block, live.astype(jnp.int32)]).astype(jnp.int32)
    terms = layer_tiles(pairs, h, (sibling, near, near_other, far, far_other))
    terms = lax.all_to_all(terms.reshape(8, -1, BLOCK, BLOCK), "layer", 0, 0)
    return jnp.sum(terms.astype(f32), axis=0)


def solution(mesh):
    return jax.shard_map(
        shards,
        mesh=mesh,
        in_specs=(P("layer", "dp", None), P("layer"), P("dp", None)),
        out_specs=P(("dp", "layer"), None, None),
        check_vma=False,
    )
```

time: 983 us -> 203 us (0.21)
  waiting for transfers between devices: 538 us -> 63 us
  other arithmetic: 270 us -> 5.62 us
  local copies, waits for them, and re-layouts: 74.6 us -> 2.1 us
  matrix products: 70.6 us -> 0 us
  Pallas kernels: 0 us -> 53.4 us
  starting transfers between devices: 6.58 us -> 47.6 us
  blocking collectives: 0 us -> 30.9 us
  between operations: 19.7 us -> 0.84 us
    psum x1 -> x0, waiting for transfers between devices: 300 us -> none  [shards(): summed = lax.psum(local_cov, 'dp')]
    another operation x33 -> x2, other arithmetic: 257 us -> 0.09 us  [the longest x1 0.08 us: shards(): place = jnp.stack([mine_x, mine_z, core]).astype(jnp.int32)]
    reduce_scatter x1 -> x0, waiting for transfers between devices: 90 us -> none  [shards(): return lax.psum_scatter(products, 'layer', scatter_dimension=0, tiled=True)]
    ppermute x4 -> x18, waiting for transfers between devices: 148 us -> 63 us  [move(): return lax.ppermute(value, 'dp', pairs)]
    pallas_call x0 -> x3, Pallas kernels: none -> 53.4 us  [the longest x1 37.8 us: solve(): pl.pallas_call(solve_kernel, out_shape=jax.ShapeDtypeStruct((DOC_DEV // B...]
    another operation x29 -> x0, matrix products: 51.2 us -> none  [the longest x14 28.8 us: shards(): factor = jnp.linalg.cholesky(covariance)]
    ppermute x4 -> x18, starting transfers between devices: 6.54 us -> 47.6 us  [move(): return lax.ppermute(value, 'dp', pairs)]
    another operation x67 -> x0, local copies, waits for them, and re-layouts: 35.8 us -> none
  transfers between devices with their start and end apart: 6 -> 18, of which waited for: 6 -> 7; matrix products, arithmetic and copies ran while one was open for 1% -> 3% of each run, Pallas kernels for 0% -> 19%
where the time goes in v1:
time: 203 us
  waiting for transfers between devices  63 us (31%)
  Pallas kernels  53.4 us (26%)
  starting transfers between devices  47.6 us (23%)
  blocking collectives  30.9 us (15%)
  other arithmetic  5.62 us (3%)
  local copies, waits for them, and re-layouts  2.1 us (1%)
    ppermute x18, waiting for transfers between devices, move(): return lax.ppermute(value, 'dp', pairs)  63 us
    ppermute x18, starting transfers between devices, move(): return lax.ppermute(value, 'dp', pairs)  47.6 us
    pallas_call x1, Pallas kernels, solve(): pl.pallas_call(solve_kernel, out_shape=jax.ShapeDtypeStruct((DOC_DEV // B...  37.8 us
    all_to_all x1, blocking collectives, shards(): terms = lax.all_to_all(terms.reshape(8, -1, BLOCK, BLOCK), 'layer', 0, 0)  30.9 us
    pallas_call x1, Pallas kernels, layer_tiles(): pl.pallas_call(tiles_kernel, out_shape=jax.ShapeDtypeStruct((count, BLOCK...  13.9 us
  transfers between devices with their start and end apart: 18, of which 7 were waited for; matrix products, arithmetic and copies ran while one was open for 3% of the time, Pallas kernels for 19%

profile of v1, /device:TPU:1, one launch (start us, length us, event | category | flops | bytes accessed | tf_op | source)
XLA Modules:
  0.0 203.4 jit_solution(5899053031573253667)
XLA Ops:
  0.0 3.2 %collective-permute-start = (bf16[512,1024]{1,0:T(8,128)(2,1)}, bf16[512,1024]{1,0:T(8,128)(2,1)S(1)}, u32[]{:S(2)}, u32[]{:S(2)}) collective-permute-start(bf16[512,1024]{1,0:T(8,128)(2,1)} %bitcast.20), channel_id=1, source_target_pairs={{0,8},{8,0},{16,24},{24,16},{32,40},{40,32},{48,56},{56,48},{64,72... | collective-permute-start | bytes 3145736 | tf_op jit(solution)/shard_map/ppermute | solution.py:45
  3.2 6.5 %collective-permute-start.14 = (bf16[512,1024]{1,0:T(8,128)(2,1)}, bf16[512,1024]{1,0:T(8,128)(2,1)}, u32[]{:S(2)}, u32[]{:S(2)}) collective-permute-start(bf16[512,1024]{1,0:T(8,128)(2,1)} %bitcast.21), channel_id=1, source_target_pairs={{0,240},{8,248},{16,0},{24,8},{32,16},{40,24},{48,32},{56,40},{64,... | collective-permute-start | bytes 3145736 | tf_op jit(solution)/shard_map/ppermute | solution.py:45
  10.4 1.2 copy-done
  11.6 1.7 shard_map.73
  13.5 1.7 collective-permute-start.2
  16.1 13.2 %collective-permute-done.1 = f32[576,128]{1,0:T(8,128)S(1)} collective-permute-done((f32[576,128]{1,0:T(8,128)S(1)}, f32[576,128]{1,0:T(8,128)S(1)}, u32[]{:S(2)}, u32[]{:S(2)}) %collective-permute-start.1) | collective-permute-done | bytes 294944 | tf_op jit(solution)/shard_map/ppermute | solution.py:45
  29.8 1.1 add_add_fusion
  31.0 9.1 %collective-permute-start.5 = (f32[144,128]{1,0:T(8,128)S(1)}, f32[144,128]{1,0:T(8,128)S(1)}, u32[]{:S(2)}, u32[]{:S(2)}) collective-permute-start(f32[144,128]{1,0:T(8,128)S(1)} %get-tuple-element.12), channel_id=1, source_target_pairs={{0,32},{8,40},{16,48},{24,56},{32,0},{40,8},{48,16},{56,24},{64,96... | collective-permute-start | bytes 221192 | tf_op jit(solution)/shard_map/ppermute | solution.py:45
  40.1 2.6 %collective-permute-done.5 = f32[144,128]{1,0:T(8,128)S(1)} collective-permute-done((f32[144,128]{1,0:T(8,128)S(1)}, f32[144,128]{1,0:T(8,128)S(1)}, u32[]{:S(2)}, u32[]{:S(2)}) %collective-permute-start.5) | collective-permute-done | bytes 73760 | tf_op jit(solution)/shard_map/ppermute | solution.py:45
  42.7 10.5 %collective-permute-done.6 = f32[144,128]{1,0:T(8,128)S(1)} collective-permute-done((f32[144,128]{1,0:T(8,128)S(1)}, f32[144,128]{1,0:T(8,128)S(1)}, u32[]{:S(2)}, u32[]{:S(2)}) %collective-permute-start.6) | collective-permute-done | bytes 73760 | tf_op jit(solution)/shard_map/ppermute | solution.py:45
  53.3 3.6 %collective-permute-start.7 = (f32[144,128]{1,0:T(8,128)S(1)}, f32[144,128]{1,0:T(8,128)S(1)}, u32[]{:S(2)}, u32[]{:S(2)}) collective-permute-start(f32[144,128]{1,0:T(8,128)S(1)} %get-tuple-element.6), channel_id=1, source_target_pairs={{0,48},{8,56},{16,0},{24,8},{32,16},{40,24},{48,32},{56,40},{64,11... | collective-permute-start | bytes 221192 | tf_op jit(solution)/shard_map/ppermute | solution.py:45
  56.9 3.2 %collective-permute-start.8 = (f32[144,128]{1,0:T(8,128)S(1)}, f32[144,128]{1,0:T(8,128)S(1)}, u32[]{:S(2)}, u32[]{:S(2)}) collective-permute-start(f32[144,128]{1,0:T(8,128)S(1)} %get-tuple-element.6), channel_id=1, source_target_pairs={{0,32},{8,40},{16,48},{24,56},{32,0},{40,8},{48,16},{56,24},{64,96... | collective-permute-start | bytes 221192 | tf_op jit(solution)/shard_map/ppermute | solution.py:45
  60.5 9.1 %collective-permute-start.16 = (bf16[512,1024]{1,0:T(8,128)(2,1)}, bf16[512,1024]{1,0:T(8,128)(2,1)}, u32[]{:S(2)}, u32[]{:S(2)}) collective-permute-start(bf16[512,1024]{1,0:T(8,128)(2,1)} %collective-permute-done.14.refs_1_), channel_id=1, source_target_pairs={{0,240},{8,248},{16,0},{24,8},{32,16},{40,24},{48,32},{56,40},{64,... | collective-permute-start | bytes 3145736 | tf_op jit(solution)/shard_map/ppermute | solution.py:45
  69.7 5.2 %collective-permute-start.10 = (f32[576,128]{1,0:T(8,128)S(1)}, f32[576,128]{1,0:T(8,128)S(1)}, u32[]{:S(2)}, u32[]{:S(2)}) collective-permute-start(f32[576,128]{1,0:T(8,128)S(1)} %pad_maximum_fusion), channel_id=1, source_target_pairs={{0,192},{8,200},{16,208},{24,216},{32,224},{40,232},{48,240},{56,2... | collective-permute-start | bytes 884744 | tf_op jit(solution)/shard_map/ppermute | solution.py:45
  75.7 6.7 %collective-permute-done.10 = f32[576,128]{1,0:T(8,128)S(1)} collective-permute-done((f32[576,128]{1,0:T(8,128)S(1)}, f32[576,128]{1,0:T(8,128)S(1)}, u32[]{:S(2)}, u32[]{:S(2)}) %collective-permute-start.10) | collective-permute-done | bytes 294944 | tf_op jit(solution)/shard_map/ppermute | solution.py:45
  82.5 7.9 %collective-permute-done.12 = f32[576,128]{1,0:T(8,128)S(1)} collective-permute-done((f32[576,128]{1,0:T(8,128)S(1)}, f32[576,128]{1,0:T(8,128)S(1)}, u32[]{:S(2)}, u32[]{:S(2)}) %collective-permute-start.12) | collective-permute-done | bytes 294944 | tf_op jit(solution)/shard_map/ppermute | solution.py:45
  90.4 1.9 collective-permute-start.13
  93.8 2.6 %fusion = s32[1,64]{1,0:T(1,128)S(1)} fusion(s32[64,2]{0,1:T(2,128)S(1)} %copy-done.2, s32[]{:T(128)} %bitcast.1, s32[]{:T(128)} %bitcast.2, s32[]{:T(128)} %bitcast.4, s32[]{:T(128)} %bitcast.3, s32[]{:T(128)S(6)} %axis_index.15), kind=kLoop, calls=%fused_computation.30 | loop fusion | flops 2496 | bytes 532 | tf_op jit(solution)/shard_map/add | solution.py:269
  96.5 21.6 %collective-permute-done.16.refs_3_ = bf16[512,1024]{1,0:T(8,128)(2,1)} collective-permute-done((bf16[512,1024]{1,0:T(8,128)(2,1)}, bf16[512,1024]{1,0:T(8,128)(2,1)}, u32[]{:S(2)}, u32[]{:S(2)}) %collective-permute-start.16) | collective-permute-done | bytes 1048608 | tf_op jit(solution)/shard_map/ppermute | solution.py:45
  118.0 1.6 collective-permute-start.17
  119.6 37.8 %shard_map.74.h_ref = bf16[4,256,1024]{2,1,0:T(8,128)(2,1)S(1)} custom-call(s32[3]{0:T(128)S(1)} %pad_add_fusion.1.place_ref, s32[1]{0:T(128)S(6)} %copy.14.level_ref, f32[2304,128]{1,0:T(8,128)S(1)} %constant_dynamic-update-slice_fusion.w_ref, f32[2304,128]{1,0:T(8,128)} %collective-permute-done.13.s_ref, bf16[512,1024]{1,0:T(8,128)(2,1)S(1)} %bitcast.23), custom_call_target="tpu_custom_call" | custom-call | flops 40000000000 | bytes 8388608 | tf_op jit(solution)/shard_map/pallas_call | solution.py:185
  157.5 13.9 %shard_map.75 = bf16[64,128,128]{2,1,0:T(8,128)(2,1)S(1)} custom-call(s32[3,64]{1,0:T(4,128)S(1)} %pad_add_fusion.pairs_ref, bf16[4,256,1024]{2,1,0:T(8,128)(2,1)S(1)} %shard_map.74.h_ref, bf16[512,1024]{1,0:T(8,128)(2,1)S(1)} %collective-permute-done.s_ref.refs_0_, bf16[512,1024]{1,0:T(8,128)(2,1)} %collective-permute-done.14.refs_1_, ...), custom_call_target="tpu_custom_call" | custom-call | flops 4294967296 | bytes 9437184 | tf_op jit(solution)/shard_map/pallas_call | solution.py:229
  171.4 30.9 %all_to_all.5 = bf16[8,8,128,128]{3,2,1,0:T(8,128)(2,1)S(1)} all-to-all(bf16[8,8,128,128]{3,2,1,0:T(8,128)(2,1)S(1)} %bitcast.19), channel_id=1, replica_groups=mesh['dp'=32,'layer'=8] {'layer'}, dimensions={0} | all-to-all | bytes 4194304 | tf_op jit(solution)/shard_map/all_to_all | solution.py:272
  202.3 1.2 convert_reduce_fusion
  (44 shorter events, 4.8 us)
Async XLA Ops:
  0.0 10.4 %collective-permute-start = (bf16[512,1024]{1,0:T(8,128)(2,1)}, bf16[512,1024]{1,0:T(8,128)(2,1)S(1)}, u32[]{:S(2)}, u32[]{:S(2)}) collective-permute-start(bf16[512,1024]{1,0:T(8,128)(2,1)} %bitcast.20), channel_id=1, source_target_pairs={{0,8},{8,0},{16,24},{24,16},{32,40},{40,32},{48,56},{56,48},{64,72... | collective-permute-start | bytes 3145736 | tf_op jit(solution)/shard_map/ppermute | solution.py:45
  3.2 57.3 %collective-permute-start.14 = (bf16[512,1024]{1,0:T(8,128)(2,1)}, bf16[512,1024]{1,0:T(8,128)(2,1)}, u32[]{:S(2)}, u32[]{:S(2)}) collective-permute-start(bf16[512,1024]{1,0:T(8,128)(2,1)} %bitcast.21), channel_id=1, source_target_pairs={{0,240},{8,248},{16,0},{24,8},{32,16},{40,24},{48,32},{56,40},{64,... | collective-permute-start | bytes 3145736 | tf_op jit(solution)/shard_map/ppermute | solution.py:45
  10.4 1.2 copy-start
  13.4 15.9 %collective-permute-start.1 = (f32[576,128]{1,0:T(8,128)S(1)}, f32[576,128]{1,0:T(8,128)S(1)}, u32[]{:S(2)}, u32[]{:S(2)}) collective-permute-start(f32[576,128]{1,0:T(8,128)S(1)} %get-tuple-element.7), channel_id=1, source_target_pairs={{0,64},{8,72},{16,80},{24,88},{32,96},{40,104},{48,112},{56,120},{... | collective-permute-start | bytes 884744 | tf_op jit(solution)/shard_map/ppermute | solution.py:45
  13.5 15.9 %collective-permute-start.2 = (f32[576,128]{1,0:T(8,128)S(1)}, f32[576,128]{1,0:T(8,128)}, u32[]{:S(2)}, u32[]{:S(2)}) collective-permute-start(f32[576,128]{1,0:T(8,128)S(1)} %get-tuple-element.9), channel_id=1, source_target_pairs={{0,128},{8,136},{16,144},{24,152},{32,160},{40,168},{48,176},{56,1... | collective-permute-start | bytes 884744 | tf_op jit(solution)/shard_map/ppermute | solution.py:45
  15.2 14.6 %collective-permute-start.3 = (f32[576,128]{1,0:T(8,128)S(1)}, f32[576,128]{1,0:T(8,128)}, u32[]{:S(2)}, u32[]{:S(2)}) collective-permute-start(f32[576,128]{1,0:T(8,128)S(1)} %get-tuple-element.8), channel_id=1, source_target_pairs={{0,192},{8,200},{16,208},{24,216},{32,224},{40,232},{48,240},{56,2... | collective-permute-start | bytes 884744 | tf_op jit(solution)/shard_map/ppermute | solution.py:45
  30.9 9.2 %collective-permute-start.4 = (f32[144,128]{1,0:T(8,128)S(1)}, f32[144,128]{1,0:T(8,128)S(1)}, u32[]{:S(2)}, u32[]{:S(2)}) collective-permute-start(f32[144,128]{1,0:T(8,128)S(1)} %get-tuple-element.10), channel_id=1, source_target_pairs={{0,16},{8,24},{16,32},{24,40},{32,48},{40,56},{48,0},{56,8},{64,80... | collective-permute-start | bytes 221192 | tf_op jit(solution)/shard_map/ppermute | solution.py:45
  31.0 11.7 %collective-permute-start.5 = (f32[144,128]{1,0:T(8,128)S(1)}, f32[144,128]{1,0:T(8,128)S(1)}, u32[]{:S(2)}, u32[]{:S(2)}) collective-permute-start(f32[144,128]{1,0:T(8,128)S(1)} %get-tuple-element.12), channel_id=1, source_target_pairs={{0,32},{8,40},{16,48},{24,56},{32,0},{40,8},{48,16},{56,24},{64,96... | collective-permute-start | bytes 221192 | tf_op jit(solution)/shard_map/ppermute | solution.py:45
  40.1 13.2 %collective-permute-start.6 = (f32[144,128]{1,0:T(8,128)S(1)}, f32[144,128]{1,0:T(8,128)S(1)}, u32[]{:S(2)}, u32[]{:S(2)}) collective-permute-start(f32[144,128]{1,0:T(8,128)S(1)} %get-tuple-element.11), channel_id=1, source_target_pairs={{0,48},{8,56},{16,0},{24,8},{32,16},{40,24},{48,32},{56,40},{64,11... | collective-permute-start | bytes 221192 | tf_op jit(solution)/shard_map/ppermute | solution.py:45
  53.3 16.3 %collective-permute-start.7 = (f32[144,128]{1,0:T(8,128)S(1)}, f32[144,128]{1,0:T(8,128)S(1)}, u32[]{:S(2)}, u32[]{:S(2)}) collective-permute-start(f32[144,128]{1,0:T(8,128)S(1)} %get-tuple-element.6), channel_id=1, source_target_pairs={{0,48},{8,56},{16,0},{24,8},{32,16},{40,24},{48,32},{56,40},{64,11... | collective-permute-start | bytes 221192 | tf_op jit(solution)/shard_map/ppermute | solution.py:45
  56.9 12.7 %collective-permute-start.8 = (f32[144,128]{1,0:T(8,128)S(1)}, f32[144,128]{1,0:T(8,128)S(1)}, u32[]{:S(2)}, u32[]{:S(2)}) collective-permute-start(f32[144,128]{1,0:T(8,128)S(1)} %get-tuple-element.6), channel_id=1, source_target_pairs={{0,32},{8,40},{16,48},{24,56},{32,0},{40,8},{48,16},{56,24},{64,96... | collective-permute-start | bytes 221192 | tf_op jit(solution)/shard_map/ppermute | solution.py:45
  60.0 9.6 %collective-permute-start.9 = (f32[144,128]{1,0:T(8,128)S(1)}, f32[144,128]{1,0:T(8,128)S(1)}, u32[]{:S(2)}, u32[]{:S(2)}) collective-permute-start(f32[144,128]{1,0:T(8,128)S(1)} %get-tuple-element.6), channel_id=1, source_target_pairs={{0,16},{8,24},{16,32},{24,40},{32,48},{40,56},{48,0},{56,8},{64,80... | collective-permute-start | bytes 221192 | tf_op jit(solution)/shard_map/ppermute | solution.py:45
  60.5 57.5 %collective-permute-start.16 = (bf16[512,1024]{1,0:T(8,128)(2,1)}, bf16[512,1024]{1,0:T(8,128)(2,1)}, u32[]{:S(2)}, u32[]{:S(2)}) collective-permute-start(bf16[512,1024]{1,0:T(8,128)(2,1)} %collective-permute-done.14.refs_1_), channel_id=1, source_target_pairs={{0,240},{8,248},{16,0},{24,8},{32,16},{40,24},{48,32},{56,40},{64,... | collective-permute-start | bytes 3145736 | tf_op jit(solution)/shard_map/ppermute | solution.py:45
  69.6 22.7 %copy-start.3 = (s32[4]{0:T(128)S(1)}, s32[4]{0:T(128)}, u32[]{:S(2)}) copy-start(s32[4]{0:T(128)} %constant.140.clone) | copy-start | bytes 52
  69.6 24.1 %copy-start.2 = (s32[64,2]{0,1:T(2,128)S(1)}, s32[64,2]{0,1:T(2,128)}, u32[]{:S(2)}) copy-start(s32[64,2]{0,1:T(2,128)} %param.9) | copy-start | bytes 1540
  69.7 50.0 %copy-start.1 = (bf16[1,512,1024]{2,1,0:T(8,128)(2,1)S(1)}, bf16[1,512,1024]{2,1,0:T(8,128)(2,1)}, u32[]{:S(2)}) copy-start(bf16[1,512,1024]{2,1,0:T(8,128)(2,1)} %param.7) | copy-start | bytes 3145732
  69.7 12.8 %collective-permute-start.10 = (f32[576,128]{1,0:T(8,128)S(1)}, f32[576,128]{1,0:T(8,128)S(1)}, u32[]{:S(2)}, u32[]{:S(2)}) collective-permute-start(f32[576,128]{1,0:T(8,128)S(1)} %pad_maximum_fusion), channel_id=1, source_target_pairs={{0,192},{8,200},{16,208},{24,216},{32,224},{40,232},{48,240},{56,2... | collective-permute-start | bytes 884744 | tf_op jit(solution)/shard_map/ppermute | solution.py:45
  74.8 7.7 %collective-permute-start.11 = (f32[576,128]{1,0:T(8,128)S(1)}, f32[576,128]{1,0:T(8,128)S(1)}, u32[]{:S(2)}, u32[]{:S(2)}) collective-permute-start(f32[576,128]{1,0:T(8,128)S(1)} %pad_maximum_fusion), channel_id=1, source_target_pairs={{0,128},{8,136},{16,144},{24,152},{32,160},{40,168},{48,176},{56,1... | collective-permute-start | bytes 884744 | tf_op jit(solution)/shard_map/ppermute | solution.py:45
  75.2 15.2 %collective-permute-start.12 = (f32[576,128]{1,0:T(8,128)S(1)}, f32[576,128]{1,0:T(8,128)S(1)}, u32[]{:S(2)}, u32[]{:S(2)}) collective-permute-start(f32[576,128]{1,0:T(8,128)S(1)} %pad_maximum_fusion), channel_id=1, source_target_pairs={{0,64},{8,72},{16,80},{24,88},{32,96},{40,104},{48,112},{56,120},{... | collective-permute-start | bytes 884744 | tf_op jit(solution)/shard_map/ppermute | solution.py:45
  90.4 29.2 %collective-permute-start.13 = (f32[2304,128]{1,0:T(8,128)S(1)}, f32[2304,128]{1,0:T(8,128)}, u32[]{:S(2)}, u32[]{:S(2)}) collective-permute-start(f32[2304,128]{1,0:T(8,128)S(1)} %constant_dynamic-update-slice_fusion.w_ref), channel_id=1, source_target_pairs={{0,8},{8,0},{16,24},{24,16},{32,40},{40,32},{48,56},{56,48},{64,72... | collective-permute-start | bytes 3538952 | tf_op jit(solution)/shard_map/ppermute | solution.py:45
  96.4 61.1 %collective-permute-start.15 = (bf16[512,1024]{1,0:T(8,128)(2,1)}, bf16[512,1024]{1,0:T(8,128)(2,1)S(1)}, u32[]{:S(2)}, u32[]{:S(2)}) collective-permute-start(bf16[512,1024]{1,0:T(8,128)(2,1)} %collective-permute-done.14.refs_1_), channel_id=1, source_target_pairs={{0,8},{8,0},{16,24},{24,16},{32,40},{40,32},{48,56},{56,48},{64,72... | collective-permute-start | bytes 3145736 | tf_op jit(solution)/shard_map/ppermute | solution.py:45
  118.0 39.4 %collective-permute-start.17 = (bf16[512,1024]{1,0:T(8,128)(2,1)}, bf16[512,1024]{1,0:T(8,128)(2,1)S(1)}, u32[]{:S(2)}, u32[]{:S(2)}) collective-permute-start(bf16[512,1024]{1,0:T(8,128)(2,1)} %collective-permute-done.16.refs_3_), channel_id=1, source_target_pairs={{0,8},{8,0},{16,24},{24,16},{32,40},{40,32},{48,56},{56,48},{64,72... | collective-permute-start | bytes 3145736 | tf_op jit(solution)/shard_map/ppermute | solution.py:45
